TPU v7x, 32 devices: a whole 2x2x4 slice. The times are simulated.
32 devices in a mesh: dp: 16 (over z, y, x), tensor: 2 (over core).
Axes of the slice: x: 2, y: 2, z: 4, core: 2. Of those that a mesh axis runs over, the one named last changes fastest.
Arguments:
- features: bfloat16 [2048, 4096], P('dp', 'tensor'), may hold values from -6 to 6
- out_grad: bfloat16 [2048, 14336], P('dp', 'tensor'), may hold values from -0.125 to 0.125
- weight: bfloat16 [4096, 14336], P('dp', 'tensor'), may hold values from -2 to 2
- basis: bfloat16 [4096, 128], replicated, may hold values from -0.09375 to 0.09375
- moment_one: float32 [2, 7168, 128], P('tensor', 'dp'), may hold values from -3 to 3
- moment_two: float32 [2, 7168, 128], P('tensor', 'dp'), may hold values from 0.05 to 1
Outputs:
- feature_grad: bfloat16 [2048, 4096], P('dp', 'tensor')
- new_moment_one: float32 [2, 7168, 128], P('tensor', 'dp')
- new_moment_two: float32 [2, 7168, 128], P('tensor', 'dp')
- direction: float32 [2, 7168, 4096], P('tensor', 'dp')
All inputs are finite; a program needn't handle non-finite values.
Results may differ from a plain program's by a relative error of at most 0.017.
Values may be sent and summed in bfloat16 or wider, within the bound.
A program may use at most 128 MiB of HBM per device.

v0:
```python
import jax
import jax.numpy as jnp
from jax import lax
from jax.sharding import PartitionSpec as P

beta_one = 0.9
beta_two = 0.95
bias_one = 1.0 - 0.9**20
bias_two = 1.0 - 0.95**20
adam_epsilon = 1e-08


def body(features, out_grad, weight, basis, moment_one, moment_two):
    partial_value = jnp.einsum(
        "tf,df->td",
        out_grad,
        lax.all_gather(weight, "dp", axis=0, tiled=True),
        preferred_element_type=jnp.float32,
    )
    feature_grad = lax.psum_scatter(
        partial_value.astype(jnp.bfloat16), "tensor", scatter_dimension=1, tiled=True
    )
    part_width = features.shape[1]
    basis_part = lax.dynamic_slice_in_dim(
        basis, lax.axis_index("tensor") * part_width, part_width, 0
    )
    local_coords = jnp.dot(features, basis_part, preferred_element_type=jnp.float32)
    coords = lax.psum(local_coords, "tensor")
    coords = coords.astype(jnp.bfloat16)
    projected = lax.psum_scatter(
        jnp.einsum("tf,tr->fr", out_grad, coords, preferred_element_type=jnp.float32),
        "dp",
        scatter_dimension=0,
        tiled=True,
    )
    first = moment_one[0]
    second = moment_two[0]
    new_one = beta_one * first + (1.0 - beta_one) * projected
    new_two = beta_two * second + (1.0 - beta_two) * projected * projected
    step_dir = (new_one / bias_one / (jnp.sqrt(new_two / bias_two) + adam_epsilon)).astype(
        jnp.bfloat16
    )
    direction = jnp.einsum("cr,dr->cd", step_dir, basis, preferred_element_type=jnp.float32)
    return (feature_grad, new_one[None], new_two[None], direction[None])


def solution(mesh):
    in_specs = (
        P("dp", "tensor"),
        P("dp", "tensor"),
        P("dp", "tensor"),
        P(),
        P("tensor", "dp", None),
        P("tensor", "dp", None),
    )
    out_specs = (
        P("dp", "tensor"),
        P("tensor", "dp", None),
        P("tensor", "dp", None),
        P("tensor", "dp", None),
    )
    return jax.shard_map(body, mesh=mesh, in_specs=in_specs, out_specs=out_specs, check_vma=False)
```

profile of v0, /device:TPU:1, one launch (start us, length us, event | category | flops | bytes accessed | tf_op | source)
XLA Modules:
  0.0 704.7 jit_solution(13397946816842320355)
XLA Ops:
  7.2 0.0 all-gather.2.cloned.1.call-start
  7.2 0.7 all-gather.2.cloned.1.call-update
  7.9 0.0 reduce-scatter.7.cloned.1.call-start
  8.0 0.4 copy-done.4
  8.4 0.3 copy-done.2
  8.7 0.3 convolution_bitcast_fusion.2
  9.0 3.6 psum.7
  12.7 2.5 convolution_bitcast_fusion
  15.1 5.2 copy.18
  20.4 0.0 reduce-scatter.7.cloned.1.call-update
  20.4 0.0 reduce-scatter.5.cloned.1.call-start
  20.4 580.7 %all-gather.2.cloned.1.call-done = bf16[4096,7168]{1,0:T(8,128)(2,1)} async-done(((bf16[256,7168]{1,0:T(8,128)(2,1)}), bf16[4096,7168]{1,0:T(8,128)(2,1)}) %all-gather.2.cloned.1.call-update) | async-done | bytes 58720272 | tf_op jit(solution)/shard_map/all_gather | solution.py:17
  601.1 26.2 %convolution_convert_fusion = bf16[128,4096]{1,0:T(8,128)(2,1)} fusion(bf16[128,7168]{1,0:T(8,128)(2,1)S(1)} %copy-done, bf16[4096,7168]{1,0:T(8,128)(2,1)} %all-gather.2.cloned.1.call-done), kind=kOutput, calls=%fused_computation.2 | convolution fusion | flops 7516717056 | bytes 61603840 | tf_op jit(solution)/shard_map/tf,df->td/dot_general | solution.py:14
  627.3 0.0 reduce-scatter.5.cloned.1.call-update
  627.3 0.1 copy.15
  627.5 1.1 copy.14
  628.6 57.5 %reduce-scatter.7.cloned.1.call-done = f32[448,128]{1,0:T(8,128)} async-done(((f32[7168,128]{1,0:T(8,128)}), f32[448,128]{1,0:T(8,128)}) %reduce-scatter.7.cloned.1.call-update) | async-done | bytes 229392
  686.1 1.1 copy.19
  687.1 0.7 copy-done.3
  687.8 0.8 fusion.7
  688.6 0.8 copy.16
  689.5 1.9 copy.17
  691.4 5.2 convolution_bitcast_fusion.1
  696.6 1.6 reduce-scatter.5.cloned.1.call-done
  (9 shorter events, 0.0 us)
Async XLA Ops:
  7.2 5.5 copy-start
  7.2 1.2 copy-start.4
  7.2 1.5 copy-start.2
  7.2 593.9 %all-gather.2.cloned.1.call-start = ((), (), s32[]{:S(2)}) async-start(), calls=%async_computation.2 | async-start | bytes 62390272 | tf_op jit(solution)/shard_map/all_gather | solution.py:17
  7.9 678.1 %reduce-scatter.7.cloned.1.call-start = ((), (), s32[]{:S(2)}) async-start(), calls=%async_computation.4 | async-start | bytes 3899392
  20.4 606.9 %copy-start.5 = (f32[1,448,128]{2,1,0:T(8,128)S(1)}, f32[1,448,128]{2,1,0:T(8,128)}, u32[]{:S(2)}) copy-start(f32[1,448,128]{2,1,0:T(8,128)} %param.11) | copy-start | bytes 688132
  20.4 677.8 %reduce-scatter.5.cloned.1.call-start = ((), (), s32[]{:S(2)}) async-start(), calls=%async_computation.3 | async-start | bytes 1572864 | tf_op jit(solution)/shard_map/reduce_scatter | solution.py:20
  687.1 0.7 copy-start.3
  689.4 8.7 %copy-start.1 = (bf16[128,7168]{1,0:T(8,128)(2,1)S(1)}, bf16[128,7168]{1,0:T(8,128)(2,1)}, u32[]{:S(2)}) copy-start(bf16[128,7168]{1,0:T(8,128)(2,1)} %param.7) | copy-start | bytes 5505028
Sparse Core Ops, SparseCore 0:
  10.8 590.3 all-gather.1
  603.4 82.5 reduce-scatter.6
  688.9 9.2 reduce-scatter.4
where the time goes:
time: 706 us; the launch traced here: 705 us
  waiting for transfers between devices  640 us (91%)
  matrix products  34.2 us (5%)
  between operations  13.8 us (2%)
  local copies, waits for them, and re-layouts  11.6 us (2%)
    all_gather x1, waiting for transfers between devices, body(): lax.all_gather(weight, 'dp', axis=0, tiled=True)  581 us
    unnamed x4, waiting for transfers between devices  58.2 us
    dot_general x1, matrix products, body(): jnp.einsum('tf,df->td', out_grad, lax.all_gather(weight, 'dp', axis=0, ti...  26.2 us
  transfers between devices with their start and end apart: 3, of which 3 were waited for; matrix products, arithmetic and copies ran while one was open for 6% of the time, Pallas kernels for 0%

commit v1 on v0

--- a/solution.py
+++ b/solution.py
@@ -1,6 +1,10 @@
+import functools
+
 import jax
 import jax.numpy as jnp
 from jax import lax
+from jax.experimental import pallas as pl
+from jax.experimental.pallas import tpu as pltpu
 from jax.sharding import PartitionSpec as P
 
 beta_one = 0.9
@@ -9,8 +13,408 @@
 bias_two = 1.0 - 0.95**20
 adam_epsilon = 1e-08
 
-
-def body(features, out_grad, weight, basis, moment_one, moment_two):
+MESH = pl.DeviceIdType.MESH
+SQUARE = 4
+PARTS = 2
+LANES = 1024
+NT = (((1,), (1,)), ((), ()))
+TN = (((0,), (0,)), ((), ()))
+
+
+def exchange_kernel(
+    line, n_tensor,
+    features, out_grad, weight, basis,
+    grad_out, projected_out,
+    tokens, rows, coords, coords_part, tiles, pair_tiles, final_tiles, proj, proj_send, proj_recv,
+    local_sem, line_send, line_recv, row_send, row_recv, far_send, far_recv,
+    part_send, part_recv, coords_send, coords_recv,
+    proj_send_sem, proj_recv_sem, pair_send, pair_recv, final_send, final_recv,
+):
+    me = lax.axis_index("dp")
+    core = lax.axis_index("tensor")
+    place = me // SQUARE
+    corner = me % SQUARE
+    side_x = place * SQUARE + corner + 1 - 2 * (corner % 2)
+    side_y = place * SQUARE + corner + 2 - 4 * (corner // 2)
+    far = place * SQUARE + (SQUARE - 1 - corner)
+    other = 1 - core
+    n_tok = out_grad.shape[0]
+    width = out_grad.shape[1]
+    n_row = weight.shape[0]
+    half = n_row // 2
+    piece = n_tok // PARTS
+    own = line // n_tensor
+
+    def on_line(z):
+        return z * SQUARE + corner
+
+    def remote(src, dst, send, recv, dp, tensor):
+        return pltpu.make_async_remote_copy(
+            src_ref=src, dst_ref=dst, send_sem=send, recv_sem=recv,
+            device_id=(dp, tensor), device_id_type=MESH,
+        )
+
+    def arrived(dst, sem):
+        remote(dst, dst, sem, sem, me, other).wait_recv()
+
+    def token_piece(z, p):
+        return tokens.at[pl.ds(pl.multiple_of(z * n_tok + p * piece, piece), piece), :]
+
+    keep_tokens = pltpu.make_async_copy(
+        out_grad, tokens.at[pl.ds(pl.multiple_of(place * n_tok, n_tok), n_tok), :], local_sem.at[0]
+    )
+    keep_rows = pltpu.make_async_copy(weight, rows.at[0], local_sem.at[1])
+    keep_tokens.start()
+    keep_rows.start()
+
+    barrier = pltpu.get_barrier_semaphore()
+    greeted = [(me, other), (side_x, core), (side_y, core), (far, core)]
+    for s in range(1, line):
+        for t in range(n_tensor):
+            greeted.append((on_line((place + s) % line), t))
+    for dp, t in greeted:
+        pl.semaphore_signal(barrier, inc=1, device_id=(dp, t), device_id_type=MESH)
+    pl.semaphore_wait(barrier, len(greeted))
+
+    def line_copy(src, z, p, way):
+        target = on_line(place + 1 if way == 0 else place - 1)
+        return remote(
+            src, token_piece(z, p), line_send.at[way, z, p], line_recv.at[z, p], target, core
+        )
+
+    for p in range(PARTS):
+        for way, there in ((0, place + 1 < line), (1, place > 0)):
+            @pl.when(there)
+            def _():
+                line_copy(out_grad.at[pl.ds(p * piece, piece), :], place, p, way).start()
+
+    def row_copy(slot, h):
+        return remote(
+            weight.at[pl.ds(h * half, half), :],
+            rows.at[slot, pl.ds(h * half, half), :],
+            row_send.at[slot - 1, h], row_recv.at[slot - 1, h],
+            side_x if slot == 1 else side_y, core,
+        )
+
+    def far_copy(h):
+        src = rows.at[1 + h, pl.ds(h * half, half), :]
+        return remote(
+            src, rows.at[3, pl.ds(h * half, half), :], far_send.at[h], far_recv.at[h],
+            side_y if h == 0 else side_x, core,
+        )
+
+    for slot, h in ((1, 0), (2, 1), (1, 1), (2, 0)):
+        row_copy(slot, h).start()
+
+    depth = features.shape[1]
+    coords_part[0] = jnp.dot(
+        features[...],
+        basis[pl.ds(pl.multiple_of(core * depth, depth), depth), :],
+        preferred_element_type=jnp.float32,
+    )
+    part_copy = remote(
+        coords_part.at[0], coords_part.at[1], part_send.at[0], part_recv.at[0], me, other
+    )
+    part_copy.start()
+    part_copy.wait()
+    coords[place] = (coords_part[0] + coords_part[1]).astype(coords.dtype)
+
+    def coords_copy(s):
+        z = (place + s) % line
+        return remote(
+            coords.at[place], coords.at[place], coords_send.at[s], coords_recv.at[place],
+            on_line(z), core,
+        )
+
+    for s in range(1, line):
+        coords_copy(s).start()
+    keep_tokens.wait()
+    keep_rows.wait()
+
+    strip = SQUARE * projected_out.shape[0]
+
+    def add_projected(z, first=False):
+        block = tokens[
+            pl.ds(pl.multiple_of(z * n_tok, n_tok), n_tok),
+            pl.ds(pl.multiple_of(place * strip, strip), strip),
+        ]
+        term = lax.dot_general(block, coords[z], TN, preferred_element_type=jnp.float32)
+        proj[...] = term if first else proj[...] + term
+
+    def product(first_token, count, slot):
+        def step(k, total):
+            at = pl.ds(pl.multiple_of(k * LANES, LANES), LANES)
+            return total + lax.dot_general(
+                tokens[pl.ds(first_token, count), at], rows[slot, :, at], NT,
+                preferred_element_type=jnp.float32,
+            )
+
+        start = jnp.zeros((count, n_row), jnp.float32)
+        return lax.fori_loop(0, width // LANES, step, start)
+
+    def column(slot):
+        flip_x = slot % 2
+        flip_y = slot // 2
+        x, y = corner % 2, corner // 2
+        return (x + flip_x) % 2 + 2 * ((y + flip_y) % 2)
+
+    def tile(z, slot):
+        got = product(pl.multiple_of(z * n_tok, n_tok), n_tok, slot)
+        tiles[z, column(slot)] = got.astype(tiles.dtype)
+
+    def tiles_of(z, slots):
+        def one(slot, carry):
+            tile(z, slot)
+            return carry
+
+        lax.fori_loop(slots[0], slots[1], one, 0)
+
+    add_projected(place, first=True)
+    tile(place, 0)
+
+    late = max(line - 2, 1)
+    for s in range(1, line):
+        from_left = place - s >= 0
+        from_right = place + s < line
+        for p in range(PARTS):
+            for way, here, z, on in (
+                (0, from_left, place - s, place + 1 < line),
+                (1, from_right, place + s, place > 0),
+            ):
+                @pl.when(here)
+                def _():
+                    arrived(token_piece(z, p), line_recv.at[z, p])
+
+                    @pl.when(on)
+                    def _():
+                        line_copy(token_piece(z, p), z, p, way).start()
+
+        if s == 1:
+            for h in range(2):
+                arrived(rows.at[1 + h, pl.ds(h * half, half), :], row_recv.at[h, h])
+                far_copy(h).start()
+
+        for here, z in ((from_left, place - s), (from_right, place + s)):
+            @pl.when(here)
+            def _():
+                arrived(coords.at[z], coords_recv.at[z])
+                add_projected(z)
+
+        if s == line - 1:
+            for r in range(SQUARE):
+                proj_send[r] = proj[
+                    pl.ds(r * projected_out.shape[0], projected_out.shape[0]), :
+                ].astype(proj_send.dtype)
+            for r, dp in ((1, side_x), (2, side_y), (3, far)):
+                remote(
+                    proj_send.at[dp - place * SQUARE], proj_recv.at[r - 1],
+                    proj_send_sem.at[r - 1], proj_recv_sem.at[r - 1], dp, core,
+                ).start()
+
+        for here, z in ((from_left, place - s), (from_right, place + s)):
+            @pl.when(here)
+            def _():
+                tiles_of(z, (0, 3 if s > late else 1))
+
+        if s == late:
+            for h in range(2):
+                arrived(
+                    rows.at[1 + h, pl.ds((1 - h) * half, half), :], row_recv.at[h, 1 - h]
+                )
+
+            def early(z, carry):
+                @pl.when((z - place <= late) & (place - z <= late))
+                def _():
+                    tiles_of(z, (1, 3))
+
+                return carry
+
+            lax.fori_loop(0, line, early, 0)
+
+    for h in range(2):
+        arrived(rows.at[3, pl.ds(h * half, half), :], far_recv.at[h])
+
+    def last(z, carry):
+        tile(z, 3)
+        return carry
+
+    def last_other(i, carry):
+        return last(other * own + i, carry)
+
+    def last_own(i, carry):
+        return last(core * own + i, carry)
+
+    pair_copies = [
+        remote(
+            tiles.at[other * own + i], pair_tiles.at[i], pair_send.at[i], pair_recv.at[i], me, other
+        )
+        for i in range(own)
+    ]
+    lax.fori_loop(0, own, last_other, 0)
+    for copy in pair_copies:
+        copy.start()
+    lax.fori_loop(0, own, last_own, 0)
+
+    mine = place // own
+    for i in range(own):
+        pair_copies[i].wait_recv()
+        z = core * own + i
+        pair_tiles[i] = (
+            tiles[z].astype(jnp.float32) + pair_tiles[i].astype(jnp.float32)
+        ).astype(pair_tiles.dtype)
+
+        @pl.when(z == place)
+        def _():
+            final_tiles[place % own] = pair_tiles[i]
+
+        @pl.when(z != place)
+        def _():
+            remote(
+                pair_tiles.at[i], final_tiles.at[place % own],
+                final_send.at[i], final_recv.at[place % own], on_line(z), mine,
+            ).start()
+
+    count = projected_out.shape[0]
+    total = proj[pl.ds(pl.multiple_of(corner * count, count), count), :]
+    for r in range(3):
+        arrived(proj_recv.at[r], proj_recv_sem.at[r])
+        total = total + proj_recv[r].astype(jnp.float32)
+    projected_out[...] = total
+
+    for i in range(own):
+        @pl.when(core * own + i != place)
+        def _():
+            arrived(final_tiles.at[i], final_recv.at[i])
+
+        for c in range(SQUARE):
+            at = (i * SQUARE + c) * n_row
+            grad_out[:, pl.ds(at, n_row)] = final_tiles[i, c]
+
+    for s in range(1, line):
+        coords_copy(s).wait_send()
+    for slot in (1, 2):
+        for h in range(2):
+            row_copy(slot, h).wait_send()
+    for h in range(2):
+        far_copy(h).wait_send()
+    for s in range(line):
+        for p in range(PARTS):
+            for way, here, z, on in (
+                (0, place - s >= 0, place - s, place + 1 < line),
+                (1, place + s < line, place + s, place > 0),
+            ):
+                @pl.when(here & on)
+                def _():
+                    line_copy(token_piece(z, p), z, p, way).wait_send()
+    for r, dp in ((1, side_x), (2, side_y), (3, far)):
+        remote(
+            proj_send.at[dp - place * SQUARE], proj_recv.at[r - 1],
+            proj_send_sem.at[r - 1], proj_recv_sem.at[r - 1], dp, core,
+        ).wait_send()
+    for i in range(own):
+        pair_copies[i].wait_send()
+
+        @pl.when(core * own + i != place)
+        def _():
+            remote(
+                pair_tiles.at[i], final_tiles.at[place % own],
+                final_send.at[i], final_recv.at[place % own], on_line(core * own + i), mine,
+            ).wait_send()
+
+
+def adam_kernel(projected, moment_one, moment_two, basis, new_one, new_two, direction, step_dir):
+    @pl.when(pl.program_id(0) == 0)
+    def _():
+        value = projected[...]
+        one = beta_one * moment_one[...] + (1.0 - beta_one) * value
+        two = beta_two * moment_two[...] + (1.0 - beta_two) * value * value
+        new_one[...] = one
+        new_two[...] = two
+        step_dir[...] = (
+            one / bias_one / (jnp.sqrt(two / bias_two) + adam_epsilon)
+        ).astype(step_dir.dtype)
+
+    direction[...] = lax.dot_general(
+        step_dir[...], basis[...], NT, preferred_element_type=jnp.float32
+    )
+
+
+def fused_body(n_dp, n_tensor, features, out_grad, weight, basis, moment_one, moment_two):
+    line = n_dp // SQUARE
+    own = line // n_tensor
+    n_tok, width = out_grad.shape
+    n_row = weight.shape[0]
+    units, rank = moment_one.shape[1:]
+    dma = pltpu.SemaphoreType.DMA
+    bf16, f32 = jnp.bfloat16, jnp.float32
+    feature_grad, projected = pl.pallas_call(
+        functools.partial(exchange_kernel, line, n_tensor),
+        out_shape=(
+            jax.ShapeDtypeStruct(features.shape, bf16),
+            jax.ShapeDtypeStruct((units, rank), f32),
+        ),
+        in_specs=[
+            pl.BlockSpec(memory_space=pltpu.VMEM),
+            pl.BlockSpec(memory_space=pl.ANY),
+            pl.BlockSpec(memory_space=pl.ANY),
+            pl.BlockSpec(memory_space=pltpu.VMEM),
+        ],
+        out_specs=[pl.BlockSpec(memory_space=pltpu.VMEM)] * 2,
+        scratch_shapes=[
+            pltpu.VMEM((line * n_tok, width), bf16),
+            pltpu.VMEM((SQUARE, n_row, width), bf16),
+            pltpu.VMEM((line, n_tok, rank), bf16),
+            pltpu.VMEM((2, n_tok, rank), f32),
+            pltpu.VMEM((line, SQUARE, n_tok, n_row), bf16),
+            pltpu.VMEM((own, SQUARE, n_tok, n_row), bf16),
+            pltpu.VMEM((own, SQUARE, n_tok, n_row), bf16),
+            pltpu.VMEM((SQUARE * units, rank), f32),
+            pltpu.VMEM((SQUARE, units, rank), bf16),
+            pltpu.VMEM((SQUARE - 1, units, rank), bf16),
+            dma((2,)),
+            dma((2, line, PARTS)),
+            dma((line, PARTS)),
+            dma((2, 2)),
+            dma((2, 2)),
+            dma((2,)),
+            dma((2,)),
+            dma((1,)),
+            dma((1,)),
+            dma((line,)),
+            dma((line,)),
+            dma((SQUARE - 1,)),
+            dma((SQUARE - 1,)),
+            dma((own,)),
+            dma((own,)),
+            dma((own,)),
+            dma((own,)),
+        ],
+        compiler_params=pltpu.CompilerParams(
+            collective_id=0, has_side_effects=True, vmem_limit_bytes=48 << 20
+        ),
+        name="exchange",
+    )(features, out_grad, weight, basis)
+
+    n_feature = basis.shape[0]
+    block = min(512, n_feature)
+    whole = pl.BlockSpec((units, rank), lambda i: (0, 0))
+    new_one, new_two, direction = pl.pallas_call(
+        adam_kernel,
+        grid=(n_feature // block,),
+        out_shape=(
+            jax.ShapeDtypeStruct((units, rank), f32),
+            jax.ShapeDtypeStruct((units, rank), f32),
+            jax.ShapeDtypeStruct((units, n_feature), f32),
+        ),
+        in_specs=[whole, whole, whole, pl.BlockSpec((block, rank), lambda i: (i, 0))],
+        out_specs=[whole, whole, pl.BlockSpec((units, block), lambda i: (0, i))],
+        scratch_shapes=[pltpu.VMEM((units, rank), bf16)],
+        name="adam",
+    )(projected, moment_one[0], moment_two[0], basis)
+    return (feature_grad, new_one[None], new_two[None], direction[None])
+
+
+def gathered_body(features, out_grad, weight, basis, moment_one, moment_two):
     partial_value = jnp.einsum(
         "tf,df->td",
         out_grad,
@@ -44,6 +448,25 @@
     return (feature_grad, new_one[None], new_two[None], direction[None])
 
 
+def body(n_dp, n_tensor, *arrays):
+    features, out_grad, weight, _, moment_one, _ = arrays
+    line = n_dp // SQUARE
+    units = moment_one.shape[1]
+    fits = (
+        n_tensor == 2
+        and n_dp % SQUARE == 0
+        and line % n_tensor == 0
+        and out_grad.shape[1] % LANES == 0
+        and out_grad.shape[0] % (16 * PARTS) == 0
+        and weight.shape[0] % 128 == 0
+        and units % 16 == 0
+        and (units * SQUARE) % 128 == 0
+    )
+    if fits:
+        return fused_body(n_dp, n_tensor, *arrays)
+    return gathered_body(*arrays)
+
+
 def solution(mesh):
     in_specs = (
         P("dp", "tensor"),
@@ -59,4 +482,5 @@
         P("tensor", "dp", None),
         P("tensor", "dp", None),
     )
-    return jax.shard_map(body, mesh=mesh, in_specs=in_specs, out_specs=out_specs, check_vma=False)
+    run = functools.partial(body, mesh.shape["dp"], mesh.shape["tensor"])
+    return jax.shard_map(run, mesh=mesh, in_specs=in_specs, out_specs=out_specs, check_vma=False)

time: 706 us -> 165 us (0.23)
  waiting for transfers between devices: 640 us -> 0 us
  Pallas kernels: 0 us -> 159 us
  matrix products: 34.2 us -> 0 us
  between operations: 13.8 us -> 0.66 us
    all_gather x1 -> x0, waiting for transfers between devices: 581 us -> none  [body(): lax.all_gather(weight, 'dp', axis=0, tiled=True)]
    pallas_call x0 -> x2, Pallas kernels: none -> 159 us  [the longest x1 151 us: fused_body(): pl.pallas_call(functools.partial(exchange_kernel, line, n_tensor), out_sh...]
    unnamed x4 -> x0, waiting for transfers between devices: 58.2 us -> none
    dot_general x4 -> x0, matrix products: 34.2 us -> none  [the longest x1 26.2 us: body(): jnp.einsum('tf,df->td', out_grad, lax.all_gather(weight, 'dp', axis=0, ti...]
  transfers between devices with their start and end apart: 3 -> 0, of which waited for: 3 -> 0; matrix products, arithmetic and copies ran while one was open for 6% -> 0% of each run, Pallas kernels for 0% -> 0%
where the time goes in v1:
time: 165 us
  Pallas kernels  159 us (96%)
  local copies, waits for them, and re-layouts  5.24 us (3%)
    pallas_call x1, Pallas kernels, fused_body(): pl.pallas_call(functools.partial(exchange_kernel, line, n_tensor), out_sh...  151 us
    pallas_call x1, Pallas kernels, fused_body(): pl.pallas_call(adam_kernel, grid=(n_feature // block,), out_shape=(jax.Sh...  7.62 us
    unnamed x9, local copies, waits for them, and re-layouts  5.24 us

profile of v1, /device:TPU:1, one launch (start us, length us, event | category | flops | bytes accessed | tf_op | source)
XLA Modules:
  0.0 164.7 jit_solution(1712038482169897673)
XLA Ops:
  0.6 0.0 copy-start
  0.6 1.2 copy-done
  1.9 0.0 copy-start.1
  1.9 1.5 copy-done.1
  3.4 0.0 copy-start.2
  3.4 1.0 copy-done.2
  4.4 151.1 %exchange.1 = (bf16[128,2048]{1,0:T(8,128)(2,1)S(1)}, f32[448,128]{1,0:T(8,128)S(1)}) custom-call(bf16[128,2048]{1,0:T(8,128)(2,1)S(1)} %copy-done.2, bf16[128,7168]{1,0:T(8,128)(2,1)S(1)} %copy-done.1, bf16[256,7168]{1,0:T(8,128)(2,1)} %weight.1, bf16[4096,128]{1,0:T(8,128)(2,1)S(1)} %copy-done), custom_call_target="tpu_custom_call" | custom-call | tf_op jit(solution)/shard_map/exchange/pallas_call | solution.py:350
  155.6 0.0 copy-start.3
  155.6 0.7 copy-done.3
  156.2 7.6 %adam.1 = (f32[448,128]{1,0:T(8,128)}, f32[448,128]{1,0:T(8,128)}, f32[448,4096]{1,0:T(8,128)}) custom-call(f32[448,128]{1,0:T(8,128)} %copy-done.3, f32[448,128]{1,0:T(8,128)} %bitcast.5, f32[448,128]{1,0:T(8,128)} %bitcast.6, bf16[4096,128]{1,0:T(8,128)(2,1)} %basis.3), custom_call_target="tpu_custom_call" | custom-call | tf_op jit(solution)/shard_map/adam/pallas_call | solution.py:401
  163.9 0.8 copy.11
Async XLA Ops:
  0.6 1.2 copy-start
  1.9 1.5 copy-start.1
  3.4 1.0 copy-start.2
  155.6 0.7 copy-start.3

commit v2 on v1

--- a/solution.py
+++ b/solution.py
@@ -21,11 +21,18 @@
 TN = (((0,), (0,)), ((), ()))
 
 
+def moments(projected, moment_one, moment_two):
+    return (
+        beta_one * moment_one + (1.0 - beta_one) * projected,
+        beta_two * moment_two + (1.0 - beta_two) * projected * projected,
+    )
+
+
 def exchange_kernel(
     line, n_tensor,
-    features, out_grad, weight, basis,
-    grad_out, projected_out,
-    tokens, rows, coords, coords_part, tiles, pair_tiles, final_tiles, proj, proj_send, proj_recv,
+    features_in, out_grad, weight, basis_in, moment_one_in, moment_two_in,
+    grad_out, projected_out, step_out,
+    features, basis, moment_one, moment_two, tokens, rows, coords, coords_part, tiles, pair_tiles, final_tiles, proj, proj_send, proj_recv,
     local_sem, line_send, line_recv, row_send, row_recv, far_send, far_recv,
     part_send, part_recv, coords_send, coords_recv,
     proj_send_sem, proj_recv_sem, pair_send, pair_recv, final_send, final_recv,
@@ -41,7 +48,7 @@
     n_tok = out_grad.shape[0]
     width = out_grad.shape[1]
     n_row = weight.shape[0]
-    half = n_row // 2
+    quarter = n_row // 4
     piece = n_tok // PARTS
     own = line // n_tensor
 
@@ -64,8 +71,23 @@
         out_grad, tokens.at[pl.ds(pl.multiple_of(place * n_tok, n_tok), n_tok), :], local_sem.at[0]
     )
     keep_rows = pltpu.make_async_copy(weight, rows.at[0], local_sem.at[1])
+    loads = [
+        pltpu.make_async_copy(src, dst, local_sem.at[2 + i])
+        for i, (src, dst) in enumerate(
+            (
+                (features_in, features),
+                (basis_in, basis),
+                (moment_one_in, moment_one),
+                (moment_two_in, moment_two),
+            )
+        )
+    ]
+    for load in loads[:2]:
+        load.start()
     keep_tokens.start()
     keep_rows.start()
+    for load in loads[2:]:
+        load.start()
 
     barrier = pltpu.get_barrier_semaphore()
     greeted = [(me, other), (side_x, core), (side_y, core), (far, core)]
@@ -88,25 +110,27 @@
             def _():
                 line_copy(out_grad.at[pl.ds(p * piece, piece), :], place, p, way).start()
 
-    def row_copy(slot, h):
+    def row_copy(slot, k):
         return remote(
-            weight.at[pl.ds(h * half, half), :],
-            rows.at[slot, pl.ds(h * half, half), :],
-            row_send.at[slot - 1, h], row_recv.at[slot - 1, h],
+            weight.at[pl.ds(k * quarter, quarter), :],
+            rows.at[slot, pl.ds(k * quarter, quarter), :],
+            row_send.at[slot - 1, k], row_recv.at[slot - 1, k],
             side_x if slot == 1 else side_y, core,
         )
 
-    def far_copy(h):
-        src = rows.at[1 + h, pl.ds(h * half, half), :]
+    def far_copy(k):
+        src = rows.at[1 + k // 2, pl.ds(k * quarter, quarter), :]
         return remote(
-            src, rows.at[3, pl.ds(h * half, half), :], far_send.at[h], far_recv.at[h],
-            side_y if h == 0 else side_x, core,
-        )
-
-    for slot, h in ((1, 0), (2, 1), (1, 1), (2, 0)):
-        row_copy(slot, h).start()
+            src, rows.at[3, pl.ds(k * quarter, quarter), :], far_send.at[k], far_recv.at[k],
+            side_y if k < 2 else side_x, core,
+        )
+
+    for slot, k in ((1, 0), (2, 2), (1, 1), (2, 3), (1, 2), (2, 0)):
+        row_copy(slot, k).start()
 
     depth = features.shape[1]
+    loads[0].wait()
+    loads[1].wait()
     coords_part[0] = jnp.dot(
         features[...],
         basis[pl.ds(pl.multiple_of(core * depth, depth), depth), :],
@@ -190,9 +214,13 @@
                         line_copy(token_piece(z, p), z, p, way).start()
 
         if s == 1:
-            for h in range(2):
-                arrived(rows.at[1 + h, pl.ds(h * half, half), :], row_recv.at[h, h])
-                far_copy(h).start()
+            row_copy(1, 3).start()
+            row_copy(2, 1).start()
+        if s == late:
+            for k in (0, 2, 1, 3):
+                slot = 1 + k // 2
+                arrived(rows.at[slot, pl.ds(k * quarter, quarter), :], row_recv.at[slot - 1, k])
+                far_copy(k).start()
 
         for here, z in ((from_left, place - s), (from_right, place + s)):
             @pl.when(here)
@@ -217,10 +245,8 @@
                 tiles_of(z, (0, 3 if s > late else 1))
 
         if s == late:
-            for h in range(2):
-                arrived(
-                    rows.at[1 + h, pl.ds((1 - h) * half, half), :], row_recv.at[h, 1 - h]
-                )
+            for slot, k in ((1, 2), (2, 0), (1, 3), (2, 1)):
+                arrived(rows.at[slot, pl.ds(k * quarter, quarter), :], row_recv.at[slot - 1, k])
 
             def early(z, carry):
                 @pl.when((z - place <= late) & (place - z <= late))
@@ -231,18 +257,13 @@
 
             lax.fori_loop(0, line, early, 0)
 
-    for h in range(2):
-        arrived(rows.at[3, pl.ds(h * half, half), :], far_recv.at[h])
-
-    def last(z, carry):
-        tile(z, 3)
-        return carry
-
-    def last_other(i, carry):
-        return last(other * own + i, carry)
-
-    def last_own(i, carry):
-        return last(core * own + i, carry)
+    for k in range(4):
+        arrived(rows.at[3, pl.ds(k * quarter, quarter), :], far_recv.at[k])
+
+    def last(t):
+        got = product(pl.multiple_of(t * own * n_tok, own * n_tok), own * n_tok, 3)
+        for i in range(own):
+            tiles[t * own + i, column(3)] = got[i * n_tok : (i + 1) * n_tok].astype(tiles.dtype)
 
     pair_copies = [
         remote(
@@ -250,10 +271,10 @@
         )
         for i in range(own)
     ]
-    lax.fori_loop(0, own, last_other, 0)
+    last(other)
     for copy in pair_copies:
         copy.start()
-    lax.fori_loop(0, own, last_own, 0)
+    last(core)
 
     mine = place // own
     for i in range(own):
@@ -280,6 +301,12 @@
         arrived(proj_recv.at[r], proj_recv_sem.at[r])
         total = total + proj_recv[r].astype(jnp.float32)
     projected_out[...] = total
+    loads[2].wait()
+    loads[3].wait()
+    one, two = moments(total, moment_one[...], moment_two[...])
+    step_out[...] = (
+        one / bias_one / (jnp.sqrt(two / bias_two) + adam_epsilon)
+    ).astype(step_out.dtype)
 
     for i in range(own):
         @pl.when(core * own + i != place)
@@ -293,10 +320,10 @@
     for s in range(1, line):
         coords_copy(s).wait_send()
     for slot in (1, 2):
-        for h in range(2):
-            row_copy(slot, h).wait_send()
-    for h in range(2):
-        far_copy(h).wait_send()
+        for k in range(4):
+            row_copy(slot, k).wait_send()
+    for k in range(4):
+        far_copy(k).wait_send()
     for s in range(line):
         for p in range(PARTS):
             for way, here, z, on in (
@@ -322,21 +349,14 @@
             ).wait_send()
 
 
-def adam_kernel(projected, moment_one, moment_two, basis, new_one, new_two, direction, step_dir):
-    @pl.when(pl.program_id(0) == 0)
-    def _():
-        value = projected[...]
-        one = beta_one * moment_one[...] + (1.0 - beta_one) * value
-        two = beta_two * moment_two[...] + (1.0 - beta_two) * value * value
-        new_one[...] = one
-        new_two[...] = two
-        step_dir[...] = (
-            one / bias_one / (jnp.sqrt(two / bias_two) + adam_epsilon)
-        ).astype(step_dir.dtype)
-
+def direction_kernel(step_dir, projected, moment_one, moment_two, basis, new_one, new_two, direction):
     direction[...] = lax.dot_general(
         step_dir[...], basis[...], NT, preferred_element_type=jnp.float32
     )
+
+    @pl.when(pl.program_id(0) == 1)
+    def _():
+        new_one[...], new_two[...] = moments(projected[...], moment_one[...], moment_two[...])
 
 
 def fused_body(n_dp, n_tensor, features, out_grad, weight, basis, moment_one, moment_two):
@@ -347,20 +367,20 @@
     units, rank = moment_one.shape[1:]
     dma = pltpu.SemaphoreType.DMA
     bf16, f32 = jnp.bfloat16, jnp.float32
-    feature_grad, projected = pl.pallas_call(
+    feature_grad, projected, step_dir = pl.pallas_call(
         functools.partial(exchange_kernel, line, n_tensor),
         out_shape=(
             jax.ShapeDtypeStruct(features.shape, bf16),
             jax.ShapeDtypeStruct((units, rank), f32),
+            jax.ShapeDtypeStruct((units, rank), bf16),
         ),
-        in_specs=[
-            pl.BlockSpec(memory_space=pltpu.VMEM),
-            pl.BlockSpec(memory_space=pl.ANY),
-            pl.BlockSpec(memory_space=pl.ANY),
-            pl.BlockSpec(memory_space=pltpu.VMEM),
-        ],
-        out_specs=[pl.BlockSpec(memory_space=pltpu.VMEM)] * 2,
+        in_specs=[pl.BlockSpec(memory_space=pltpu.HBM)] * 6,
+        out_specs=[pl.BlockSpec(memory_space=pltpu.VMEM)] * 3,
         scratch_shapes=[
+            pltpu.VMEM(features.shape, bf16),
+            pltpu.VMEM(basis.shape, bf16),
+            pltpu.VMEM((units, rank), f32),
+            pltpu.VMEM((units, rank), f32),
             pltpu.VMEM((line * n_tok, width), bf16),
             pltpu.VMEM((SQUARE, n_row, width), bf16),
             pltpu.VMEM((line, n_tok, rank), bf16),
@@ -371,13 +391,13 @@
             pltpu.VMEM((SQUARE * units, rank), f32),
             pltpu.VMEM((SQUARE, units, rank), bf16),
             pltpu.VMEM((SQUARE - 1, units, rank), bf16),
-            dma((2,)),
+            dma((6,)),
             dma((2, line, PARTS)),
             dma((line, PARTS)),
-            dma((2, 2)),
-            dma((2, 2)),
-            dma((2,)),
-            dma((2,)),
+            dma((2, 4)),
+            dma((2, 4)),
+            dma((4,)),
+            dma((4,)),
             dma((1,)),
             dma((1,)),
             dma((line,)),
@@ -390,27 +410,27 @@
             dma((own,)),
         ],
         compiler_params=pltpu.CompilerParams(
-            collective_id=0, has_side_effects=True, vmem_limit_bytes=48 << 20
+            collective_id=0, has_side_effects=True, vmem_limit_bytes=64 << 20
         ),
         name="exchange",
-    )(features, out_grad, weight, basis)
+    )(features, out_grad, weight, basis, moment_one[0], moment_two[0])
 
     n_feature = basis.shape[0]
-    block = min(512, n_feature)
+    block = n_feature // 4
     whole = pl.BlockSpec((units, rank), lambda i: (0, 0))
     new_one, new_two, direction = pl.pallas_call(
-        adam_kernel,
+        direction_kernel,
         grid=(n_feature // block,),
         out_shape=(
             jax.ShapeDtypeStruct((units, rank), f32),
             jax.ShapeDtypeStruct((units, rank), f32),
             jax.ShapeDtypeStruct((units, n_feature), f32),
         ),
-        in_specs=[whole, whole, whole, pl.BlockSpec((block, rank), lambda i: (i, 0))],
+        in_specs=[whole, whole, whole, whole, pl.BlockSpec((block, rank), lambda i: (i, 0))],
         out_specs=[whole, whole, pl.BlockSpec((units, block), lambda i: (0, i))],
-        scratch_shapes=[pltpu.VMEM((units, rank), bf16)],
-        name="adam",
-    )(projected, moment_one[0], moment_two[0], basis)
+        compiler_params=pltpu.CompilerParams(vmem_limit_bytes=64 << 20),
+        name="direction",
+    )(step_dir, projected, moment_one[0], moment_two[0], basis)
     return (feature_grad, new_one[None], new_two[None], direction[None])
 
 
@@ -449,7 +469,7 @@
 
 
 def body(n_dp, n_tensor, *arrays):
-    features, out_grad, weight, _, moment_one, _ = arrays
+    _, out_grad, weight, basis, moment_one, _ = arrays
     line = n_dp // SQUARE
     units = moment_one.shape[1]
     fits = (
@@ -460,6 +480,7 @@
         and out_grad.shape[0] % (16 * PARTS) == 0
         and weight.shape[0] % 128 == 0
         and units % 16 == 0
+        and basis.shape[0] % 512 == 0
         and (units * SQUARE) % 128 == 0
     )
     if fits:

time: 165 us -> 158 us (0.958)
  Pallas kernels: 159 us -> 154 us
  local copies, waits for them, and re-layouts: 5.24 us -> 1.88 us
    unnamed x9 -> x1, local copies, waits for them, and re-layouts: 5.24 us -> 1.88 us
    pallas_call x1, Pallas kernels: 151 us -> 149 us  [fused_body(): pl.pallas_call(functools.partial(exchange_kernel, line, n_tensor), out_sh...]
    pallas_call x1, Pallas kernels: 7.62 us -> 5.75 us  [fused_body(): pl.pallas_call(direction_kernel, grid=(n_feature // block,), out_shape=(j...]
where the time goes in v2:
time: 158 us; the launch traced here: 157 us
  Pallas kernels  154 us (97%)
  local copies, waits for them, and re-layouts  1.88 us (1%)
    pallas_call x1, Pallas kernels, fused_body(): pl.pallas_call(functools.partial(exchange_kernel, line, n_tensor), out_sh...  149 us
    pallas_call x1, Pallas kernels, fused_body(): pl.pallas_call(direction_kernel, grid=(n_feature // block,), out_shape=(j...  5.75 us

profile of v2, /device:TPU:1, one launch (start us, length us, event | category | flops | bytes accessed | tf_op | source)
XLA Modules:
  0.0 156.9 jit_solution(9312865874281856449)
XLA Ops:
  0.6 148.6 %exchange.1 = (bf16[128,2048]{1,0:T(8,128)(2,1)}, f32[448,128]{1,0:T(8,128)}, bf16[448,128]{1,0:T(8,128)(2,1)}) custom-call(bf16[128,2048]{1,0:T(8,128)(2,1)} %features_in.1, bf16[128,7168]{1,0:T(8,128)(2,1)} %out_grad.1, bf16[256,7168]{1,0:T(8,128)(2,1)} %weight.1, bf16[4096,128]{1,0:T(8,128)(2,1)} %basis.1, f32[448,128]{1,0:T(8,128)} %bitcast.5, ...), custom_call_target="tpu_custom_call" | custom-call | tf_op jit(solution)/shard_map/exchange/pallas_call | solution.py:370
  149.2 5.8 %direction.1 = (f32[448,128]{1,0:T(8,128)}, f32[448,128]{1,0:T(8,128)}, f32[448,4096]{1,0:T(8,128)}) custom-call(bf16[448,128]{1,0:T(8,128)(2,1)} %get-tuple-element.11.step_dir, f32[448,128]{1,0:T(8,128)} %get-tuple-element.12.projected, f32[448,128]{1,0:T(8,128)} %bitcast.6, f32[448,128]{1,0:T(8,128)} %bitcast.8, bf16[4096,128]{1,0:T(8,128)(2,1)} %basis.1), custom_call_target="tpu_custom_call" | custom-call | tf_op jit(solution)/shard_map/direction/pallas_call | solution.py:421
  155.0 1.9 %copy.11 = bf16[128,2048]{1,0:T(8,128)(2,1)} copy(bf16[128,2048]{1,0:T(8,128)(2,1)} %get-tuple-element.20) | data formatting | bytes 1048576

commit v3 on v2

--- a/solution.py
+++ b/solution.py
@@ -15,7 +15,7 @@
 
 MESH = pl.DeviceIdType.MESH
 SQUARE = 4
-PARTS = 2
+PARTS = 4
 LANES = 1024
 NT = (((1,), (1,)), ((), ()))
 TN = (((0,), (0,)), ((), ()))
@@ -31,8 +31,8 @@
 def exchange_kernel(
     line, n_tensor,
     features_in, out_grad, weight, basis_in, moment_one_in, moment_two_in,
-    grad_out, projected_out, step_out,
-    features, basis, moment_one, moment_two, tokens, rows, coords, coords_part, tiles, pair_tiles, final_tiles, proj, proj_send, proj_recv,
+    final_tiles, projected_out, step_out,
+    features, basis, moment_one, moment_two, tokens, rows, coords, coords_part, tiles, pair_tiles, proj, proj_send, proj_recv,
     local_sem, line_send, line_recv, row_send, row_recv, far_send, far_recv,
     part_send, part_recv, coords_send, coords_recv,
     proj_send_sem, proj_recv_sem, pair_send, pair_recv, final_send, final_recv,
@@ -104,11 +104,14 @@
             src, token_piece(z, p), line_send.at[way, z, p], line_recv.at[z, p], target, core
         )
 
-    for p in range(PARTS):
+    def send_own(p):
         for way, there in ((0, place + 1 < line), (1, place > 0)):
             @pl.when(there)
             def _():
                 line_copy(out_grad.at[pl.ds(p * piece, piece), :], place, p, way).start()
+
+    for p in range(2):
+        send_own(p)
 
     def row_copy(slot, k):
         return remote(
@@ -213,15 +216,12 @@
                     def _():
                         line_copy(token_piece(z, p), z, p, way).start()
 
+            if s == 1 and p + 2 < PARTS:
+                send_own(p + 2)
+
         if s == 1:
             row_copy(1, 3).start()
             row_copy(2, 1).start()
-        if s == late:
-            for k in (0, 2, 1, 3):
-                slot = 1 + k // 2
-                arrived(rows.at[slot, pl.ds(k * quarter, quarter), :], row_recv.at[slot - 1, k])
-                far_copy(k).start()
-
         for here, z in ((from_left, place - s), (from_right, place + s)):
             @pl.when(here)
             def _():
@@ -244,6 +244,12 @@
             def _():
                 tiles_of(z, (0, 3 if s > late else 1))
 
+        if s == 1:
+            for k in (0, 2, 1, 3):
+                slot = 1 + k // 2
+                arrived(rows.at[slot, pl.ds(k * quarter, quarter), :], row_recv.at[slot - 1, k])
+                far_copy(k).start()
+
         if s == late:
             for slot, k in ((1, 2), (2, 0), (1, 3), (2, 1)):
                 arrived(rows.at[slot, pl.ds(k * quarter, quarter), :], row_recv.at[slot - 1, k])
@@ -277,6 +283,12 @@
     last(core)
 
     mine = place // own
+
+    def keep_final(i):
+        return pltpu.make_async_copy(
+            pair_tiles.at[i], final_tiles.at[place % own], local_sem.at[0]
+        )
+
     for i in range(own):
         pair_copies[i].wait_recv()
         z = core * own + i
@@ -286,7 +298,7 @@
 
         @pl.when(z == place)
         def _():
-            final_tiles[place % own] = pair_tiles[i]
+            keep_final(i).start()
 
         @pl.when(z != place)
         def _():
@@ -313,9 +325,9 @@
         def _():
             arrived(final_tiles.at[i], final_recv.at[i])
 
-        for c in range(SQUARE):
-            at = (i * SQUARE + c) * n_row
-            grad_out[:, pl.ds(at, n_row)] = final_tiles[i, c]
+        @pl.when(core * own + i == place)
+        def _():
+            keep_final(i).wait()
 
     for s in range(1, line):
         coords_copy(s).wait_send()
@@ -349,7 +361,12 @@
             ).wait_send()
 
 
-def direction_kernel(step_dir, projected, moment_one, moment_two, basis, new_one, new_two, direction):
+def direction_kernel(
+    step_dir, projected, moment_one, moment_two, basis, tiles,
+    new_one, new_two, direction, feature_grad,
+):
+    for i in range(tiles.shape[0]):
+        feature_grad[:, pl.ds(i * tiles.shape[2], tiles.shape[2])] = tiles[i]
     direction[...] = lax.dot_general(
         step_dir[...], basis[...], NT, preferred_element_type=jnp.float32
     )
@@ -367,15 +384,19 @@
     units, rank = moment_one.shape[1:]
     dma = pltpu.SemaphoreType.DMA
     bf16, f32 = jnp.bfloat16, jnp.float32
-    feature_grad, projected, step_dir = pl.pallas_call(
+    tiles, projected, step_dir = pl.pallas_call(
         functools.partial(exchange_kernel, line, n_tensor),
         out_shape=(
-            jax.ShapeDtypeStruct(features.shape, bf16),
+            jax.ShapeDtypeStruct((own, SQUARE, n_tok, n_row), bf16),
             jax.ShapeDtypeStruct((units, rank), f32),
             jax.ShapeDtypeStruct((units, rank), bf16),
         ),
         in_specs=[pl.BlockSpec(memory_space=pltpu.HBM)] * 6,
-        out_specs=[pl.BlockSpec(memory_space=pltpu.VMEM)] * 3,
+        out_specs=[
+            pl.BlockSpec(memory_space=pl.ANY),
+            pl.BlockSpec(memory_space=pltpu.VMEM),
+            pl.BlockSpec(memory_space=pltpu.VMEM),
+        ],
         scratch_shapes=[
             pltpu.VMEM(features.shape, bf16),
             pltpu.VMEM(basis.shape, bf16),
@@ -386,7 +407,6 @@
             pltpu.VMEM((line, n_tok, rank), bf16),
             pltpu.VMEM((2, n_tok, rank), f32),
             pltpu.VMEM((line, SQUARE, n_tok, n_row), bf16),
-            pltpu.VMEM((own, SQUARE, n_tok, n_row), bf16),
             pltpu.VMEM((own, SQUARE, n_tok, n_row), bf16),
             pltpu.VMEM((SQUARE * units, rank), f32),
             pltpu.VMEM((SQUARE, units, rank), bf16),
@@ -418,19 +438,29 @@
     n_feature = basis.shape[0]
     block = n_feature // 4
     whole = pl.BlockSpec((units, rank), lambda i: (0, 0))
-    new_one, new_two, direction = pl.pallas_call(
+    count = own * SQUARE // 4
+    new_one, new_two, direction, feature_grad = pl.pallas_call(
         direction_kernel,
         grid=(n_feature // block,),
         out_shape=(
             jax.ShapeDtypeStruct((units, rank), f32),
             jax.ShapeDtypeStruct((units, rank), f32),
             jax.ShapeDtypeStruct((units, n_feature), f32),
+            jax.ShapeDtypeStruct(features.shape, bf16),
         ),
-        in_specs=[whole, whole, whole, whole, pl.BlockSpec((block, rank), lambda i: (i, 0))],
-        out_specs=[whole, whole, pl.BlockSpec((units, block), lambda i: (0, i))],
+        in_specs=[
+            whole, whole, whole, whole,
+            pl.BlockSpec((block, rank), lambda i: (i, 0)),
+            pl.BlockSpec((count, n_tok, n_row), lambda i: (i, 0, 0)),
+        ],
+        out_specs=[
+            whole, whole,
+            pl.BlockSpec((units, block), lambda i: (0, i)),
+            pl.BlockSpec((n_tok, count * n_row), lambda i: (0, i)),
+        ],
         compiler_params=pltpu.CompilerParams(vmem_limit_bytes=64 << 20),
         name="direction",
-    )(step_dir, projected, moment_one[0], moment_two[0], basis)
+    )(step_dir, projected, moment_one[0], moment_two[0], basis, tiles.reshape(own * SQUARE, n_tok, n_row))
     return (feature_grad, new_one[None], new_two[None], direction[None])
 
 

time: 158 us -> 157 us (level)
  local copies, waits for them, and re-layouts: 1.88 us -> 0 us
    unnamed x1 -> x0, local copies, waits for them, and re-layouts: 1.88 us -> none
where the time goes in v3:
time: 157 us; the launch traced here: 155 us
  Pallas kernels  155 us (99%)
    pallas_call x1, Pallas kernels, fused_body(): pl.pallas_call(functools.partial(exchange_kernel, line, n_tensor), out_sh...  149 us
    pallas_call x1, Pallas kernels, fused_body(): pl.pallas_call(direction_kernel, grid=(n_feature // block,), out_shape=(j...  6.03 us

profile of v3, /device:TPU:1, one launch (start us, length us, event | category | flops | bytes accessed | tf_op | source)
XLA Modules:
  0.0 155.3 jit_solution(18142907277518760222)
XLA Ops:
  0.6 148.7 %exchange.1 = (bf16[2,4,128,256]{3,2,1,0:T(8,128)(2,1)}, f32[448,128]{1,0:T(8,128)}, bf16[448,128]{1,0:T(8,128)(2,1)}) custom-call(bf16[128,2048]{1,0:T(8,128)(2,1)} %features_in.1, bf16[128,7168]{1,0:T(8,128)(2,1)} %out_grad.1, bf16[256,7168]{1,0:T(8,128)(2,1)} %weight.1, bf16[4096,128]{1,0:T(8,128)(2,1)} %basis.1, f32[448,128]{1,0:T(8,128)} %bitcast.6, ...), custom_call_target="tpu_custom_call" | custom-call | tf_op jit(solution)/shard_map/exchange/pallas_call | solution.py:387
  149.3 6.0 %direction.1 = (f32[448,128]{1,0:T(8,128)}, f32[448,128]{1,0:T(8,128)}, f32[448,4096]{1,0:T(8,128)}, bf16[128,2048]{1,0:T(8,128)(2,1)}) custom-call(bf16[448,128]{1,0:T(8,128)(2,1)} %get-tuple-element.11.step_dir, f32[448,128]{1,0:T(8,128)} %get-tuple-element.12.projected, f32[448,128]{1,0:T(8,128)} %bitcast.7, f32[448,128]{1,0:T(8,128)} %bitcast.9, ...), custom_call_target="tpu_custom_call" | custom-call | tf_op jit(solution)/shard_map/direction/pallas_call | solution.py:442

commit v4 on v3

--- a/solution.py
+++ b/solution.py
@@ -16,7 +16,6 @@
 MESH = pl.DeviceIdType.MESH
 SQUARE = 4
 PARTS = 4
-LANES = 1024
 NT = (((1,), (1,)), ((), ()))
 TN = (((0,), (0,)), ((), ()))
 
@@ -35,7 +34,7 @@
     features, basis, moment_one, moment_two, tokens, rows, coords, coords_part, tiles, pair_tiles, proj, proj_send, proj_recv,
     local_sem, line_send, line_recv, row_send, row_recv, far_send, far_recv,
     part_send, part_recv, coords_send, coords_recv,
-    proj_send_sem, proj_recv_sem, pair_send, pair_recv, final_send, final_recv,
+    proj_send_sem, proj_recv_sem, pair_send, pair_recv, final_send, final_recv, keep_sem,
 ):
     me = lax.axis_index("dp")
     core = lax.axis_index("tensor")
@@ -169,15 +168,10 @@
         proj[...] = term if first else proj[...] + term
 
     def product(first_token, count, slot):
-        def step(k, total):
-            at = pl.ds(pl.multiple_of(k * LANES, LANES), LANES)
-            return total + lax.dot_general(
-                tokens[pl.ds(first_token, count), at], rows[slot, :, at], NT,
-                preferred_element_type=jnp.float32,
-            )
-
-        start = jnp.zeros((count, n_row), jnp.float32)
-        return lax.fori_loop(0, width // LANES, step, start)
+        return lax.dot_general(
+            tokens[pl.ds(first_token, count), :], rows[slot], NT,
+            preferred_element_type=jnp.float32,
+        )
 
     def column(slot):
         flip_x = slot % 2
@@ -263,6 +257,52 @@
 
             lax.fori_loop(0, line, early, 0)
 
+    mine = place // own
+
+    def pair_copy(i, slot):
+        c = column(slot)
+        return remote(
+            tiles.at[other * own + i, c], pair_tiles.at[i, c],
+            pair_send.at[i, slot], pair_recv.at[i, slot], me, other,
+        )
+
+    def final_copy(i, slot):
+        c = column(slot)
+        return remote(
+            pair_tiles.at[i, c], final_tiles.at[place % own, c],
+            final_send.at[i, slot], final_recv.at[place % own, slot],
+            on_line(core * own + i), mine,
+        )
+
+    def keep_final(i, slot):
+        c = column(slot)
+        return pltpu.make_async_copy(
+            pair_tiles.at[i, c], final_tiles.at[place % own, c], keep_sem.at[slot]
+        )
+
+    def finish(slot):
+        c = column(slot)
+        for i in range(own):
+            pair_copy(i, slot).wait_recv()
+            z = core * own + i
+            pair_tiles[i, c] = (
+                tiles[z, c].astype(jnp.float32) + pair_tiles[i, c].astype(jnp.float32)
+            ).astype(pair_tiles.dtype)
+
+            @pl.when(z == place)
+            def _():
+                keep_final(i, slot).start()
+
+            @pl.when(z != place)
+            def _():
+                final_copy(i, slot).start()
+
+    for slot in range(SQUARE - 1):
+        for i in range(own):
+            pair_copy(i, slot).start()
+    for slot in range(SQUARE - 1):
+        finish(slot)
+
     for k in range(4):
         arrived(rows.at[3, pl.ds(k * quarter, quarter), :], far_recv.at[k])
 
@@ -271,41 +311,11 @@
         for i in range(own):
             tiles[t * own + i, column(3)] = got[i * n_tok : (i + 1) * n_tok].astype(tiles.dtype)
 
-    pair_copies = [
-        remote(
-            tiles.at[other * own + i], pair_tiles.at[i], pair_send.at[i], pair_recv.at[i], me, other
-        )
-        for i in range(own)
-    ]
     last(other)
-    for copy in pair_copies:
-        copy.start()
+    for i in range(own):
+        pair_copy(i, 3).start()
     last(core)
-
-    mine = place // own
-
-    def keep_final(i):
-        return pltpu.make_async_copy(
-            pair_tiles.at[i], final_tiles.at[place % own], local_sem.at[0]
-        )
-
-    for i in range(own):
-        pair_copies[i].wait_recv()
-        z = core * own + i
-        pair_tiles[i] = (
-            tiles[z].astype(jnp.float32) + pair_tiles[i].astype(jnp.float32)
-        ).astype(pair_tiles.dtype)
-
-        @pl.when(z == place)
-        def _():
-            keep_final(i).start()
-
-        @pl.when(z != place)
-        def _():
-            remote(
-                pair_tiles.at[i], final_tiles.at[place % own],
-                final_send.at[i], final_recv.at[place % own], on_line(z), mine,
-            ).start()
+    finish(3)
 
     count = projected_out.shape[0]
     total = proj[pl.ds(pl.multiple_of(corner * count, count), count), :]
@@ -321,13 +331,14 @@
     ).astype(step_out.dtype)
 
     for i in range(own):
-        @pl.when(core * own + i != place)
-        def _():
-            arrived(final_tiles.at[i], final_recv.at[i])
-
-        @pl.when(core * own + i == place)
-        def _():
-            keep_final(i).wait()
+        for slot in range(SQUARE):
+            @pl.when(core * own + i != place)
+            def _():
+                arrived(final_tiles.at[i, column(slot)], final_recv.at[i, slot])
+
+            @pl.when(core * own + i == place)
+            def _():
+                keep_final(i, slot).wait()
 
     for s in range(1, line):
         coords_copy(s).wait_send()
@@ -351,14 +362,12 @@
             proj_send_sem.at[r - 1], proj_recv_sem.at[r - 1], dp, core,
         ).wait_send()
     for i in range(own):
-        pair_copies[i].wait_send()
-
-        @pl.when(core * own + i != place)
-        def _():
-            remote(
-                pair_tiles.at[i], final_tiles.at[place % own],
-                final_send.at[i], final_recv.at[place % own], on_line(core * own + i), mine,
-            ).wait_send()
+        for slot in range(SQUARE):
+            pair_copy(i, slot).wait_send()
+
+            @pl.when(core * own + i != place)
+            def _():
+                final_copy(i, slot).wait_send()
 
 
 def direction_kernel(
@@ -424,10 +433,11 @@
             dma((line,)),
             dma((SQUARE - 1,)),
             dma((SQUARE - 1,)),
-            dma((own,)),
-            dma((own,)),
-            dma((own,)),
-            dma((own,)),
+            dma((own, SQUARE)),
+            dma((own, SQUARE)),
+            dma((own, SQUARE)),
+            dma((own, SQUARE)),
+            dma((SQUARE,)),
         ],
         compiler_params=pltpu.CompilerParams(
             collective_id=0, has_side_effects=True, vmem_limit_bytes=64 << 20
@@ -506,7 +516,7 @@
         n_tensor == 2
         and n_dp % SQUARE == 0
         and line % n_tensor == 0
-        and out_grad.shape[1] % LANES == 0
+        and out_grad.shape[1] % 256 == 0
         and out_grad.shape[0] % (16 * PARTS) == 0
         and weight.shape[0] % 128 == 0
         and units % 16 == 0

time: 157 us -> 154 us (0.981)
  Pallas kernels: 155 us -> 153 us
    pallas_call x1, Pallas kernels: 149 us -> 147 us  [fused_body(): pl.pallas_call(functools.partial(exchange_kernel, line, n_tensor), out_sh...]
where the time goes in v4:
time: 154 us
  Pallas kernels  153 us (99%)
    pallas_call x1, Pallas kernels, fused_body(): pl.pallas_call(functools.partial(exchange_kernel, line, n_tensor), out_sh...  147 us
    pallas_call x1, Pallas kernels, fused_body(): pl.pallas_call(direction_kernel, grid=(n_feature // block,), out_shape=(j...  6.03 us

profile of v4, /device:TPU:1, one launch (start us, length us, event | category | flops | bytes accessed | tf_op | source)
XLA Modules:
  0.0 153.7 jit_solution(7718151266773292581)
XLA Ops:
  0.6 147.0 %exchange.1 = (bf16[2,4,128,256]{3,2,1,0:T(8,128)(2,1)}, f32[448,128]{1,0:T(8,128)}, bf16[448,128]{1,0:T(8,128)(2,1)}) custom-call(bf16[128,2048]{1,0:T(8,128)(2,1)} %features_in.1, bf16[128,7168]{1,0:T(8,128)(2,1)} %out_grad.1, bf16[256,7168]{1,0:T(8,128)(2,1)} %weight.1, bf16[4096,128]{1,0:T(8,128)(2,1)} %basis.1, f32[448,128]{1,0:T(8,128)} %bitcast.6, ...), custom_call_target="tpu_custom_call" | custom-call | tf_op jit(solution)/shard_map/exchange/pallas_call | solution.py:396
  147.7 6.0 %direction.1 = (f32[448,128]{1,0:T(8,128)}, f32[448,128]{1,0:T(8,128)}, f32[448,4096]{1,0:T(8,128)}, bf16[128,2048]{1,0:T(8,128)(2,1)}) custom-call(bf16[448,128]{1,0:T(8,128)(2,1)} %get-tuple-element.11.step_dir, f32[448,128]{1,0:T(8,128)} %get-tuple-element.12.projected, f32[448,128]{1,0:T(8,128)} %bitcast.7, f32[448,128]{1,0:T(8,128)} %bitcast.9, ...), custom_call_target="tpu_custom_call" | custom-call | tf_op jit(solution)/shard_map/direction/pallas_call | solution.py:452

commit v5 on v4

--- a/solution.py
+++ b/solution.py
@@ -190,10 +190,73 @@
 
         lax.fori_loop(slots[0], slots[1], one, 0)
 
+    def far_tiles(z):
+        block = tokens[pl.ds(pl.multiple_of(z * n_tok, n_tok), n_tok), :]
+        got = lax.dot_general(
+            block, rows[0:3].reshape(3 * n_row, width), NT, preferred_element_type=jnp.float32
+        )
+        for slot in range(3):
+            tiles[z, column(slot)] = got[:, slot * n_row : (slot + 1) * n_row].astype(tiles.dtype)
+
     add_projected(place, first=True)
     tile(place, 0)
 
     late = max(line - 2, 1)
+    mine = place // own
+
+    def pair_copy(i, slot):
+        c = column(slot)
+        return remote(
+            tiles.at[other * own + i, c], pair_tiles.at[i, c],
+            pair_send.at[i, slot], pair_recv.at[i, slot], me, other,
+        )
+
+    def final_copy(i, slot):
+        c = column(slot)
+        return remote(
+            pair_tiles.at[i, c], final_tiles.at[place % own, c],
+            final_send.at[i, slot], final_recv.at[place % own, slot],
+            on_line(core * own + i), mine,
+        )
+
+    def keep_final(i, slot):
+        c = column(slot)
+        return pltpu.make_async_copy(
+            pair_tiles.at[i, c], final_tiles.at[place % own, c], keep_sem.at[slot]
+        )
+
+    def near(z):
+        return (z - place <= late) & (place - z <= late)
+
+    def finish(i, slot):
+        c = column(slot)
+        pair_copy(i, slot).wait_recv()
+        z = core * own + i
+        pair_tiles[i, c] = (
+            tiles[z, c].astype(jnp.float32) + pair_tiles[i, c].astype(jnp.float32)
+        ).astype(pair_tiles.dtype)
+
+        @pl.when(z == place)
+        def _():
+            keep_final(i, slot).start()
+
+        @pl.when(z != place)
+        def _():
+            final_copy(i, slot).start()
+
+    def early_slots(now):
+        for i in range(own):
+            @pl.when(near(other * own + i) == now)
+            def _():
+                for slot in range(SQUARE - 1):
+                    pair_copy(i, slot).start()
+
+        for i in range(own):
+            @pl.when(near(core * own + i) == now)
+            def _():
+                for slot in range(SQUARE - 1):
+                    finish(i, slot)
+
     for s in range(1, line):
         from_left = place - s >= 0
         from_right = place + s < line
@@ -236,7 +299,10 @@
         for here, z in ((from_left, place - s), (from_right, place + s)):
             @pl.when(here)
             def _():
-                tiles_of(z, (0, 3 if s > late else 1))
+                if s > late:
+                    far_tiles(z)
+                else:
+                    tile(z, 0)
 
         if s == 1:
             for k in (0, 2, 1, 3):
@@ -249,59 +315,16 @@
                 arrived(rows.at[slot, pl.ds(k * quarter, quarter), :], row_recv.at[slot - 1, k])
 
             def early(z, carry):
-                @pl.when((z - place <= late) & (place - z <= late))
+                @pl.when(near(z))
                 def _():
                     tiles_of(z, (1, 3))
 
                 return carry
 
             lax.fori_loop(0, line, early, 0)
-
-    mine = place // own
-
-    def pair_copy(i, slot):
-        c = column(slot)
-        return remote(
-            tiles.at[other * own + i, c], pair_tiles.at[i, c],
-            pair_send.at[i, slot], pair_recv.at[i, slot], me, other,
-        )
-
-    def final_copy(i, slot):
-        c = column(slot)
-        return remote(
-            pair_tiles.at[i, c], final_tiles.at[place % own, c],
-            final_send.at[i, slot], final_recv.at[place % own, slot],
-            on_line(core * own + i), mine,
-        )
-
-    def keep_final(i, slot):
-        c = column(slot)
-        return pltpu.make_async_copy(
-            pair_tiles.at[i, c], final_tiles.at[place % own, c], keep_sem.at[slot]
-        )
-
-    def finish(slot):
-        c = column(slot)
-        for i in range(own):
-            pair_copy(i, slot).wait_recv()
-            z = core * own + i
-            pair_tiles[i, c] = (
-                tiles[z, c].astype(jnp.float32) + pair_tiles[i, c].astype(jnp.float32)
-            ).astype(pair_tiles.dtype)
-
-            @pl.when(z == place)
-            def _():
-                keep_final(i, slot).start()
-
-            @pl.when(z != place)
-            def _():
-                final_copy(i, slot).start()
-
-    for slot in range(SQUARE - 1):
-        for i in range(own):
-            pair_copy(i, slot).start()
-    for slot in range(SQUARE - 1):
-        finish(slot)
+            early_slots(True)
+
+    early_slots(False)
 
     for k in range(4):
         arrived(rows.at[3, pl.ds(k * quarter, quarter), :], far_recv.at[k])
@@ -315,7 +338,8 @@
     for i in range(own):
         pair_copy(i, 3).start()
     last(core)
-    finish(3)
+    for i in range(own):
+        finish(i, 3)
 
     count = projected_out.shape[0]
     total = proj[pl.ds(pl.multiple_of(corner * count, count), count), :]

time: 154 us -> 151 us (0.981)
  Pallas kernels: 153 us -> 150 us
    pallas_call x1, Pallas kernels: 147 us -> 144 us  [fused_body(): pl.pallas_call(functools.partial(exchange_kernel, line, n_tensor), out_sh...]
where the time goes in v5:
time: 151 us
  Pallas kernels  150 us (99%)
    pallas_call x1, Pallas kernels, fused_body(): pl.pallas_call(functools.partial(exchange_kernel, line, n_tensor), out_sh...  144 us
    pallas_call x1, Pallas kernels, fused_body(): pl.pallas_call(direction_kernel, grid=(n_feature // block,), out_shape=(j...  6.03 us

profile of v5, /device:TPU:1, one launch (start us, length us, event | category | flops | bytes accessed | tf_op | source)
XLA Modules:
  0.0 150.8 jit_solution(15229347751433446908)
XLA Ops:
  0.6 144.1 %exchange.1 = (bf16[2,4,128,256]{3,2,1,0:T(8,128)(2,1)}, f32[448,128]{1,0:T(8,128)}, bf16[448,128]{1,0:T(8,128)(2,1)}) custom-call(bf16[128,2048]{1,0:T(8,128)(2,1)} %features_in.1, bf16[128,7168]{1,0:T(8,128)(2,1)} %out_grad.1, bf16[256,7168]{1,0:T(8,128)(2,1)} %weight.1, bf16[4096,128]{1,0:T(8,128)(2,1)} %basis.1, f32[448,128]{1,0:T(8,128)} %bitcast.6, ...), custom_call_target="tpu_custom_call" | custom-call | tf_op jit(solution)/shard_map/exchange/pallas_call | solution.py:420
  144.7 6.0 %direction.1 = (f32[448,128]{1,0:T(8,128)}, f32[448,128]{1,0:T(8,128)}, f32[448,4096]{1,0:T(8,128)}, bf16[128,2048]{1,0:T(8,128)(2,1)}) custom-call(bf16[448,128]{1,0:T(8,128)(2,1)} %get-tuple-element.11.step_dir, f32[448,128]{1,0:T(8,128)} %get-tuple-element.12.projected, f32[448,128]{1,0:T(8,128)} %bitcast.7, f32[448,128]{1,0:T(8,128)} %bitcast.9, ...), custom_call_target="tpu_custom_call" | custom-call | tf_op jit(solution)/shard_map/direction/pallas_call | solution.py:476

commit v6 on v5

--- a/solution.py
+++ b/solution.py
@@ -16,6 +16,7 @@
 MESH = pl.DeviceIdType.MESH
 SQUARE = 4
 PARTS = 4
+WINDOW = 3
 NT = (((1,), (1,)), ((), ()))
 TN = (((0,), (0,)), ((), ()))
 
@@ -109,7 +110,7 @@
             def _():
                 line_copy(out_grad.at[pl.ds(p * piece, piece), :], place, p, way).start()
 
-    for p in range(2):
+    for p in range(WINDOW):
         send_own(p)
 
     def row_copy(slot, k):
@@ -273,8 +274,8 @@
                     def _():
                         line_copy(token_piece(z, p), z, p, way).start()
 
-            if s == 1 and p + 2 < PARTS:
-                send_own(p + 2)
+            if s == 1 and p + WINDOW < PARTS:
+                send_own(p + WINDOW)
 
         if s == 1:
             row_copy(1, 3).start()

time: 151 us -> 151 us (level)
  no operation moved by 1% of the time
where the time goes in v6:
time: 151 us
  Pallas kernels  150 us (99%)
    pallas_call x1, Pallas kernels, fused_body(): pl.pallas_call(functools.partial(exchange_kernel, line, n_tensor), out_sh...  144 us
    pallas_call x1, Pallas kernels, fused_body(): pl.pallas_call(direction_kernel, grid=(n_feature // block,), out_shape=(j...  6.03 us

profile of v6, /device:TPU:1, one launch (start us, length us, event | category | flops | bytes accessed | tf_op | source)
XLA Modules:
  0.0 150.8 jit_solution(13774920502649718867)
XLA Ops:
  0.6 144.1 %exchange.1 = (bf16[2,4,128,256]{3,2,1,0:T(8,128)(2,1)}, f32[448,128]{1,0:T(8,128)}, bf16[448,128]{1,0:T(8,128)(2,1)}) custom-call(bf16[128,2048]{1,0:T(8,128)(2,1)} %features_in.1, bf16[128,7168]{1,0:T(8,128)(2,1)} %out_grad.1, bf16[256,7168]{1,0:T(8,128)(2,1)} %weight.1, bf16[4096,128]{1,0:T(8,128)(2,1)} %basis.1, f32[448,128]{1,0:T(8,128)} %bitcast.6, ...), custom_call_target="tpu_custom_call" | custom-call | tf_op jit(solution)/shard_map/exchange/pallas_call | solution.py:421
  144.7 6.0 %direction.1 = (f32[448,128]{1,0:T(8,128)}, f32[448,128]{1,0:T(8,128)}, f32[448,4096]{1,0:T(8,128)}, bf16[128,2048]{1,0:T(8,128)(2,1)}) custom-call(bf16[448,128]{1,0:T(8,128)(2,1)} %get-tuple-element.11.step_dir, f32[448,128]{1,0:T(8,128)} %get-tuple-element.12.projected, f32[448,128]{1,0:T(8,128)} %bitcast.7, f32[448,128]{1,0:T(8,128)} %bitcast.9, ...), custom_call_target="tpu_custom_call" | custom-call | tf_op jit(solution)/shard_map/direction/pallas_call | solution.py:477
